TPU v7x, 512 devices: a whole 4x4x16 slice. The times are simulated.
512 devices in a mesh: row: 16 (over y_lo, x, core), col: 32 (over y_hi, z).
Axes of the slice: x: 4, y: 4 (y_hi: 2, y_lo: 2; y = y_hi * 2 + y_lo), z: 16, core: 2. Of those that a mesh axis runs over, the one named last changes fastest.
Arguments:
- p_blocks: bfloat16 [1024, 128, 256], P(('row', 'col')), may hold values from -0.5 to 0.5
- a_blocks: bfloat16 [1024, 4096, 128], P('row', 'col'), may hold values from -6 to 6
- a_owner: int32 [16, 512], P('row', 'col'), may hold values from 0 to 31
- a_row: int32 [512, 64], P('row', 'col'), may hold values from 0 to 1
- a_count: int32 [256, 64], P('row', 'col'), may hold values from 0 to 2, as said below
Outputs:
- coarse_op: bfloat16 [256, 8192, 256], P('row', 'col')
Inputs may be any that keep to these rules, and one draw needn't show every extreme that they name: `a_count`: live blocks of one bucket are at most 2, and 2 is reached in every draw; the live load differs from tile to tile.
All inputs are finite; a program needn't handle non-finite values.
Results may differ from a plain program's by a relative error of at most 0.0049.
Values may be sent and summed in bfloat16 or wider, within the bound.
No kernel may reach another device: no remote copies, remote signals or barrier semaphores. Data moves between devices by JAX's collectives and lax.ppermute only.
A program may use at most 64 MiB of HBM per device.

v0:
```python
import jax
import jax.numpy as jnp
from jax import lax
from jax.sharding import PartitionSpec as P


def on_device(p_blocks, a_blocks, a_owner, a_row, a_count):
    groups = lax.axis_size("row")
    fine_count = p_blocks.shape[0]
    block_size = p_blocks.shape[1]
    coarse_width = p_blocks.shape[2]
    capacity = a_row.shape[1]
    panels = lax.all_gather(p_blocks, "col", axis=0, tiled=True)
    picked = a_owner.reshape(groups, 1, 1) * fine_count + a_row.reshape(
        groups, fine_count, capacity
    )
    chosen = jnp.take(panels, picked, axis=0)
    tile_blocks = a_blocks.reshape(groups, fine_count, capacity, block_size, block_size)
    slot_terms = lax.dot_general(
        tile_blocks,
        chosen,
        (((3,), (3,)), ((0, 1, 2), (0, 1, 2))),
        preferred_element_type=jnp.float32,
    )
    is_live = jnp.arange(capacity, dtype=jnp.int32)[None, None, :] < a_count[:, :, None]
    slot_terms = jnp.where(is_live[..., None, None], slot_terms, 0.0).astype(jnp.bfloat16)
    arrived = lax.all_to_all(slot_terms, "row", split_axis=0, concat_axis=0, tiled=True)
    spread = jnp.broadcast_to(
        p_blocks.reshape(fine_count, 1, block_size, coarse_width),
        (fine_count, capacity, block_size, coarse_width),
    )
    result = lax.dot_general(
        arrived, spread, (((1, 2, 3), (0, 1, 2)), ((), ())), preferred_element_type=jnp.float32
    )
    return result.astype(jnp.bfloat16)


def solution(mesh):
    in_specs = (
        P(("row", "col"), None, None),
        P("row", "col", None),
        P("row", "col"),
        P("row", "col"),
        P("row", "col"),
    )
    out_specs = P("row", "col", None)
    return jax.shard_map(
        on_device, mesh=mesh, in_specs=in_specs, out_specs=out_specs, check_vma=False
    )
```

profile of v0, /device:TPU:1, one launch (start us, length us, event | category | flops | bytes accessed | tf_op | source)
XLA Modules:
  0.0 258.3 jit_solution(17478261765161315398)
XLA Ops:
  6.5 0.0 copy-start
  6.5 0.0 all-gather.2.cloned.1.call-start
  6.5 0.7 all-gather.2.cloned.1.call-update
  7.3 0.8 reshape.50
  8.0 0.8 reshape.49
  8.8 0.8 copy.17
  9.6 0.7 multiply_bitcast_fusion
  10.2 0.1 compare_select_fusion
  10.3 0.2 copy.20
  10.5 0.1 reshape.54
  10.6 0.1 copy.18
  10.7 0.1 copy.19
  10.8 0.1 iota_compare_fusion
  10.9 161.0 %all-gather.2.cloned.1.call-done = bf16[64,128,256]{2,1,0:T(8,128)(2,1)} async-done(((bf16[2,128,256]{2,1,0:T(8,128)(2,1)}), bf16[64,128,256]{2,1,0:T(8,128)(2,1)}) %all-gather.2.cloned.1.call-update) | async-done | bytes 4194320 | tf_op jit(solution)/shard_map/all_gather | solution.py:13
  171.9 4.9 %gather_fusion = bf16[64,128,256]{2,1,0:T(8,128)(2,1)} fusion(bf16[64,128,256]{2,1,0:T(8,128)(2,1)} %all-gather.2.cloned.1.call-done, s32[1024]{0:T(1024)S(1)} %pad_clamp_fusion), kind=kCustom, calls=%fused_computation | custom fusion | bytes 8388864 | tf_op jit(solution)/shard_map/jit(_take)/gather | solution.py:17
  176.8 6.4 %copy.21 = bf16[16,2,2,128,256]{3,4,2,1,0:T(8,128)(2,1)} copy(bf16[16,2,2,128,256]{4,3,2,1,0:T(8,128)(2,1)} %bitcast.24) | data formatting | bytes 8388608 | tf_op jit(solution)/shard_map/jit(_take)/gather | solution.py:17
  183.3 0.0 copy-done
  183.3 3.5 %fusion = bf16[16,2,2,128,256]{3,4,2,1,0:T(8,128)(2,1)S(1)} fusion(pred[16,2,2]{2,1,0:T(4,128)(4,1)S(1)} %iota_compare_fusion, bf16[16,2,2,128,128]{4,3,2,1,0:T(8,128)(2,1)S(1)} %bitcast.23, bf16[16,2,2,128,256]{3,4,2,1,0:T(8,128)(2,1)} %copy.21, pred[16,2,2]{2,1,0:T(4,128)(4,1)S(1)} %copy.19), kind=kOutput, calls=%fused_computation.2 | convolution fusion | flops 543162368 | bytes 10485888 | tf_op jit(solution)/shard_map/dot_general | solution.py:19
  186.8 0.0 copy-start.1
  186.8 62.1 %all_to_all.5 = bf16[16,2,2,128,256]{3,4,2,1,0:T(8,128)(2,1)S(1)} all-to-all(bf16[16,2,2,128,256]{3,4,2,1,0:T(8,128)(2,1)S(1)} %fusion), channel_id=1, replica_groups=mesh['row'=16,'col'=32] {'row'}, dimensions={0} | all-to-all | bytes 8388608 | tf_op jit(solution)/shard_map/all_to_all | solution.py:27
  248.9 0.0 copy-done.1
  248.9 2.6 bitcast_convert_fusion
  (2 shorter events, 0.0 us)
Async XLA Ops:
  6.5 176.7 %copy-start = (bf16[64,128,128]{2,1,0:T(8,128)(2,1)S(1)}, bf16[64,128,128]{2,1,0:T(8,128)(2,1)}, u32[]{:S(2)}) copy-start(bf16[64,128,128]{2,1,0:T(8,128)(2,1)} %param.6) | copy-start | bytes 6291460
  6.5 165.4 %all-gather.2.cloned.1.call-start = ((), (), s32[]{:S(2)}) async-start(), calls=%async_computation.1 | async-start | bytes 4325376 | tf_op jit(solution)/shard_map/all_gather | solution.py:13
  186.8 62.1 %copy-start.1 = (bf16[2,128,256]{2,1,0:T(8,128)(2,1)S(1)}, bf16[2,128,256]{2,1,0:T(8,128)(2,1)}, u32[]{:S(2)}) copy-start(bf16[2,128,256]{2,1,0:T(8,128)(2,1)} %param.5) | copy-start | bytes 393220
Sparse Core Ops, SparseCore 0:
  10.5 161.3 all-gather.1
where the time goes:
time: 259 us; the launch traced here: 258 us
  waiting for transfers between devices  162 us (63%)
  blocking collectives  62.1 us (24%)
  local copies, waits for them, and re-layouts  14.2 us (5%)
  between operations  13.4 us (5%)
  matrix products  6.07 us (2%)
    all_gather x1, waiting for transfers between devices, on_device(): panels = lax.all_gather(p_blocks, 'col', axis=0, tiled=True)  161 us
    all_to_all x1, blocking collectives, on_device(): lax.all_to_all(slot_terms, 'row', split_axis=0, concat_axis=0, tiled=True)  62.1 us
    gather x2, local copies, waits for them, and re-layouts, on_device(): chosen = jnp.take(panels, picked, axis=0)  11.4 us
  transfers between devices with their start and end apart: 1, of which 1 were waited for; matrix products, arithmetic and copies ran while one was open for 1% of the time, Pallas kernels for 0%

commit v1 on v0

v1 whole, which is shorter than its diff:
```python
import functools

import jax
import jax.numpy as jnp
import numpy as np
from jax import lax
from jax.experimental import pallas as pl
from jax.experimental.pallas import tpu as pltpu
from jax.sharding import Mesh
from jax.sharding import PartitionSpec as P

AXES = ("yl", "x", "core", "yh", "z")
ROW, COL = AXES[:3], AXES[3:]
EARLY = 112
VMEM = 40 * 1024 * 1024


def params():
    return pltpu.CompilerParams(vmem_limit_bytes=VMEM)


def in_vmem():
    return pl.BlockSpec(memory_space=pltpu.VMEM)


def in_smem():
    return pl.BlockSpec(memory_space=pltpu.SMEM)


def split_kernel(p_ref, early_ref, late_ref):
    for j in range(p_ref.shape[0]):
        turned = p_ref[j].T
        if EARLY:
            early_ref[j] = turned[:EARLY]
        late_ref[j] = turned[EARLY:]


def split_panels(p):
    fine, block, width = p.shape
    late = width - EARLY
    return pl.pallas_call(
        split_kernel,
        out_shape=(
            jax.ShapeDtypeStruct((fine, EARLY, block), p.dtype),
            jax.ShapeDtypeStruct((fine, late, block), p.dtype),
        ),
        in_specs=[in_vmem()],
        out_specs=(in_vmem(), in_vmem()),
        compiler_params=params(),
    )(p)


def terms(owner_ref, row_ref, count_ref, panel, a_ref, out_ref):
    groups, _, width = out_ref.shape
    block = a_ref.shape[2]
    fine = width // block

    def bucket(s, carry):
        owner = owner_ref[0, s]
        for g in range(fine):
            count = count_ref[s, g]
            slots = []
            for m in range(2):
                found = panel(owner, row_ref[s * fine + g, m])
                slots.append(jnp.where(m < count, found, jnp.zeros_like(found)))
            total = jnp.dot(
                jnp.concatenate(slots, axis=1),
                a_ref[s * fine + g],
                preferred_element_type=jnp.float32,
            )
            out_ref[s, :, g * block : (g + 1) * block] = total.astype(out_ref.dtype)
        return carry

    lax.fori_loop(0, groups, bucket, 0, unroll=4)


def early_kernel(side, owner_ref, row_ref, count_ref, here_ref, own_ref, other_ref, a_ref, out_ref):
    fine = own_ref.shape[0] // side

    def panel(owner, row):
        at = (owner % side) * fine + row
        return jnp.where(owner // side == here_ref[0], own_ref[at], other_ref[at])

    terms(owner_ref, row_ref, count_ref, panel, a_ref, out_ref)


def late_kernel(side, planes, owner_ref, row_ref, count_ref, panels_ref, a_ref, out_ref):
    fine = panels_ref.shape[0] // (side * planes)

    def panel(owner, row):
        return panels_ref[((owner % side) * planes + owner // side) * fine + row]

    terms(owner_ref, row_ref, count_ref, panel, a_ref, out_ref)


def final_kernel(first, t_ref, p_ref, *rest):
    out_ref, held_ref, sems = rest[-3:]
    groups, rows, _ = t_ref.shape
    copies = []
    for r in range(groups):
        done = jnp.dot(t_ref[r], p_ref[...], preferred_element_type=jnp.float32)
        held_ref[r] = done.astype(held_ref.dtype)
        copy = pltpu.make_async_copy(
            held_ref.at[r], out_ref.at[r, pl.ds(first, rows), :], sems.at[r]
        )
        copy.start()
        copies.append(copy)
    for copy in copies:
        copy.wait()


def final(first, arrived, p, so_far=None):
    groups, rows, width = arrived.shape
    more = [] if so_far is None else [so_far]
    return pl.pallas_call(
        functools.partial(final_kernel, first),
        out_shape=jax.ShapeDtypeStruct((groups, p.shape[1], width), p.dtype),
        in_specs=[in_vmem(), in_vmem()] + [pl.BlockSpec(memory_space=pl.ANY)] * len(more),
        out_specs=pl.BlockSpec(memory_space=pl.ANY),
        scratch_shapes=[
            pltpu.VMEM((groups, rows, width), p.dtype),
            pltpu.SemaphoreType.DMA((groups,)),
        ],
        input_output_aliases={2: 0} if more else {},
        compiler_params=params(),
    )(arrived, p, *more)


def on_device(p, a, owner, row, count):
    groups = lax.axis_size(ROW)
    side = lax.axis_size("z")
    planes = lax.axis_size("yh")
    fine, block, width = p.shape
    stacked = a.reshape(groups * fine, -1, block)
    flat = p.reshape(fine * block, width)
    early, late = split_panels(p)

    def sent(kernel, rows, operands):
        specs = [in_smem()] * 3 + [in_smem() if x.ndim == 1 else in_vmem() for x in operands]
        summed = pl.pallas_call(
            kernel,
            out_shape=jax.ShapeDtypeStruct((groups, rows, fine * block), p.dtype),
            in_specs=specs + [in_vmem()],
            out_specs=in_vmem(),
            compiler_params=params(),
        )(owner, row, count, *operands, stacked)
        return lax.all_to_all(summed, ROW, split_axis=0, concat_axis=0, tiled=True)

    pair = lax.all_gather(late, "yh", axis=0, tiled=True)
    early, pair = lax.optimization_barrier((early, pair))
    late_panels = lax.all_gather(pair, "z", axis=0, tiled=True)
    own = lax.all_gather(early, "z", axis=0, tiled=True)
    other = lax.ppermute(own, "yh", [(0, 1), (1, 0)])
    here = lax.axis_index("yh").astype(jnp.int32).reshape(1)
    arrived = sent(functools.partial(early_kernel, side), EARLY, (here, own, other))
    result = final(0, arrived, flat)
    arrived = sent(functools.partial(late_kernel, side, planes), width - EARLY, (late_panels,))
    return final(EARLY, arrived, flat, result)


def solution(mesh):
    fine_mesh = Mesh(np.array(mesh.devices).reshape(2, 4, 2, 2, 16), AXES)
    in_specs = (
        P(AXES, None, None),
        P(ROW, COL, None),
        P(ROW, COL),
        P(ROW, COL),
        P(ROW, COL),
    )
    return jax.shard_map(
        on_device,
        mesh=fine_mesh,
        in_specs=in_specs,
        out_specs=P(ROW, COL, None),
        check_vma=False,
    )
```

time: 259 us -> 136 us (0.53)
  waiting for transfers between devices: 162 us -> 36.7 us
  starting transfers between devices: 0.01 us -> 21.9 us
  blocking collectives: 62.1 us -> 45.5 us
  Pallas kernels: 0 us -> 8.22 us
  matrix products: 6.07 us -> 0 us
  local copies, waits for them, and re-layouts: 14.2 us -> 9.35 us
    all_gather x1, waiting for transfers between devices: 161 us -> 0.01 us  [on_device(): late_panels = lax.all_gather(pair, 'z', axis=0, tiled=True)]
    all_to_all x1 -> x0, blocking collectives: 62.1 us -> none  [on_device(): lax.all_to_all(slot_terms, 'row', split_axis=0, concat_axis=0, tiled=True)]
    all_gather x0 -> x2, blocking collectives: none -> 45.5 us  [the longest x1 39.3 us: on_device(): own = lax.all_gather(early, 'z', axis=0, tiled=True)]
    all_to_all x0 -> x2, waiting for transfers between devices: none -> 25.6 us  [sent(): return lax.all_to_all(summed, ROW, split_axis=0, concat_axis=0, tiled=True)]
    all_to_all x0 -> x2, starting transfers between devices: none -> 18.3 us  [sent(): return lax.all_to_all(summed, ROW, split_axis=0, concat_axis=0, tiled=True)]
    gather x2 -> x0, local copies, waits for them, and re-layouts: 11.4 us -> none  [on_device(): chosen = jnp.take(panels, picked, axis=0)]
    ppermute x0 -> x1, waiting for transfers between devices: none -> 11.1 us  [on_device(): other = lax.ppermute(own, 'yh', [(0, 1), (1, 0)])]
    unnamed x5 -> x22, local copies, waits for them, and re-layouts: 0.78 us -> 9.35 us
  transfers between devices with their start and end apart: 1 -> 4, of which waited for: 1 -> 3; matrix products, arithmetic and copies ran while one was open for 1% -> 1% of each run, Pallas kernels for 0% -> 5%
where the time goes in v1:
time: 136 us; the launch traced here: 135 us
  blocking collectives  45.5 us (33%)
  waiting for transfers between devices  36.7 us (27%)
  starting transfers between devices  21.9 us (16%)
  between operations  13.5 us (10%)
  local copies, waits for them, and re-layouts  9.35 us (7%)
  Pallas kernels  8.22 us (6%)
    all_gather x1, blocking collectives, on_device(): own = lax.all_gather(early, 'z', axis=0, tiled=True)  39.3 us
    all_to_all x2, waiting for transfers between devices, sent(): return lax.all_to_all(summed, ROW, split_axis=0, concat_axis=0, tiled=True)  25.6 us
    all_to_all x2, starting transfers between devices, sent(): return lax.all_to_all(summed, ROW, split_axis=0, concat_axis=0, tiled=True)  18.3 us
    ppermute x1, waiting for transfers between devices, on_device(): other = lax.ppermute(own, 'yh', [(0, 1), (1, 0)])  11.1 us
    unnamed x22, local copies, waits for them, and re-layouts  9.35 us
    all_gather x1, blocking collectives, on_device(): pair = lax.all_gather(late, 'yh', axis=0, tiled=True)  6.24 us
    pallas_call x2, Pallas kernels, sent(): pl.pallas_call(kernel, out_shape=jax.ShapeDtypeStruct((groups, rows, fine...  5.53 us
    ppermute x1, starting transfers between devices, on_device(): other = lax.ppermute(own, 'yh', [(0, 1), (1, 0)])  3.63 us
  transfers between devices with their start and end apart: 4, of which 3 were waited for; matrix products, arithmetic and copies ran while one was open for 1% of the time, Pallas kernels for 5%

profile of v1, /device:TPU:1, one launch (start us, length us, event | category | flops | bytes accessed | tf_op | source)
XLA Modules:
  0.0 135.3 jit_solution(11193315128230235865)
XLA Ops:
  6.5 0.0 all-gather.2.cloned.1.call-start
  6.5 0.0 copy-start.4
  6.5 0.9 copy-done.4
  7.4 0.1 shard_map.55
  7.5 6.2 %all_gather.9 = bf16[4,144,128]{2,1,0:T(8,128)(2,1)} all-gather(bf16[2,144,128]{2,1,0:T(8,128)(2,1)S(1)} %get-tuple-element.10), channel_id=1, replica_groups=mesh['yl'=2,'x'=4,'core'=2,'yh'=2,'z'=16] {'yh'}, dimensions={0}, use_global_device_ids=true | all-gather | bytes 221184 | tf_op jit(solution)/shard_map/all_gather | solution.py:149
  13.8 0.0 all-gather.2.cloned.1.call-update
  13.8 39.3 %all_gather.11.own_ref = bf16[32,112,128]{2,1,0:T(8,128)(2,1)S(1)} all-gather(bf16[2,112,128]{2,1,0:T(8,128)(2,1)S(1)} %get-tuple-element.12), channel_id=1, replica_groups=mesh['yl'=2,'x'=4,'core'=2,'yh'=2,'z'=16] {'z'}, dimensions={0}, use_global_device_ids=true | all-gather | bytes 974848 | tf_op jit(solution)/shard_map/all_gather | solution.py:152
  53.1 3.6 %collective-permute-start = (bf16[32,112,128]{2,1,0:T(8,128)(2,1)S(1)}, bf16[32,112,128]{2,1,0:T(8,128)(2,1)S(1)}, u32[]{:S(2)}, u32[]{:S(2)}) collective-permute-start(bf16[32,112,128]{2,1,0:T(8,128)(2,1)S(1)} %all_gather.11.own_ref), channel_id=1, source_target_pairs={{0,16},{16,0},{1,17},{17,1},{2,18},{18,2},{3,19},{19,3},{4,20},{20... | collective-permute-start | bytes 2752520 | tf_op jit(solution)/shard_map/ppermute | solution.py:153
  56.7 0.8 copy.12.count_ref
  57.5 0.8 copy.11.row_ref
  58.2 11.1 %collective-permute-done.other_ref = bf16[32,112,128]{2,1,0:T(8,128)(2,1)S(1)} collective-permute-done((bf16[32,112,128]{2,1,0:T(8,128)(2,1)S(1)}, bf16[32,112,128]{2,1,0:T(8,128)(2,1)S(1)}, u32[]{:S(2)}, u32[]{:S(2)}) %collective-permute-start) | collective-permute-done | bytes 917536 | tf_op jit(solution)/shard_map/ppermute | solution.py:153
  69.4 0.0 copy-start.6
  69.4 0.9 copy-done.6
  70.3 1.6 %copy-done = bf16[64,128,128]{2,1,0:T(8,128)(2,1)S(1)} copy-done((bf16[64,128,128]{2,1,0:T(8,128)(2,1)S(1)}, bf16[64,128,128]{2,1,0:T(8,128)(2,1)}, u32[]{:S(2)}) %copy-start) | copy-done | bytes 2097176
  71.9 1.2 copy-done.7
  73.1 0.7 copy-done.8
  73.7 2.3 %shard_map.57 = bf16[16,112,256]{2,1,0:T(8,128)(2,1)S(1)} custom-call(s32[1,16]{1,0:T(1,128)S(1)} %copy-done.8, s32[32,2]{1,0:T(8,128)S(1)} %copy.11.row_ref, s32[16,2]{1,0:T(8,128)S(1)} %copy.12.count_ref, s32[1]{0:T(128)} %bitcast.2.here_ref, bf16[32,112,128]{2,1,0:T(8,128)(2,1)S(1)} %all_gather.11.own_ref, bf16[32,112,128]{2,1,0:T(8,128)(2,1)S(1)} %copy-done.7, ...), custom_call_target="tpu_custom_call" | custom-call | tf_op jit(solution)/shard_map/pallas_call | solution.py:140
  76.0 0.0 copy-start.2
  76.0 0.9 copy-done.2
  76.9 14.1 %all-to-all-start.1 = ((bf16[16,112,256]{2,1,0:T(8,128)(2,1)}), bf16[16,112,256]{2,1,0:T(8,128)(2,1)S(1)}, u32[]{:S(2)}, u32[]{:S(2)}) async-start(bf16[16,112,256]{2,1,0:T(8,128)(2,1)} %copy-done.2), calls=%async_computation.1 | async-start | bytes 1835008 | tf_op jit(solution)/shard_map/all_to_all | solution.py:147
  91.0 0.0 all-gather.2.cloned.1.call-done.panels_ref
  91.0 0.0 copy-done.1
  91.1 0.0 copy-done.9
  91.1 0.0 copy-start.3
  91.1 1.7 %copy-done.3 = bf16[64,144,128]{2,1,0:T(8,128)(2,1)S(1)} copy-done((bf16[64,144,128]{2,1,0:T(8,128)(2,1)S(1)}, bf16[64,144,128]{2,1,0:T(8,128)(2,1)}, u32[]{:S(2)}) %copy-start.3) | copy-done | bytes 2359320
  92.7 3.3 %shard_map.56 = bf16[16,144,256]{2,1,0:T(8,128)(2,1)} custom-call(s32[1,16]{1,0:T(1,128)S(1)} %copy-done.9, s32[32,2]{1,0:T(8,128)S(1)} %copy.11.row_ref, s32[16,2]{1,0:T(8,128)S(1)} %copy.12.count_ref, bf16[64,144,128]{2,1,0:T(8,128)(2,1)S(1)} %copy-done.3, bf16[32,256,128]{2,1,0:T(8,128)(2,1)S(1)} %bitcast.4), custom_call_target="tpu_custom_call" | custom-call | tf_op jit(solution)/shard_map/pallas_call | solution.py:140
  96.0 9.5 %all-to-all-done.1.t_ref = bf16[16,112,256]{2,1,0:T(8,128)(2,1)S(1)} async-done(((bf16[16,112,256]{2,1,0:T(8,128)(2,1)}), bf16[16,112,256]{2,1,0:T(8,128)(2,1)S(1)}, u32[]{:S(2)}, u32[]{:S(2)}) %all-to-all-start.1) | async-done | bytes 917536 | tf_op jit(solution)/shard_map/all_to_all | solution.py:147
  105.5 4.2 %all-to-all-start = ((bf16[16,144,256]{2,1,0:T(8,128)(2,1)}), bf16[16,144,256]{2,1,0:T(8,128)(2,1)S(1)}, u32[]{:S(2)}, u32[]{:S(2)}) async-start(bf16[16,144,256]{2,1,0:T(8,128)(2,1)} %shard_map.56), calls=%async_computation | async-start | bytes 2359296 | tf_op jit(solution)/shard_map/all_to_all | solution.py:147
  109.7 0.0 copy-done.5
  109.7 1.3 shard_map.58.rest_0_
  111.0 16.1 %all-to-all-done.t_ref = bf16[16,144,256]{2,1,0:T(8,128)(2,1)S(1)} async-done(((bf16[16,144,256]{2,1,0:T(8,128)(2,1)}), bf16[16,144,256]{2,1,0:T(8,128)(2,1)S(1)}, u32[]{:S(2)}, u32[]{:S(2)}) %all-to-all-start) | async-done | bytes 1179680 | tf_op jit(solution)/shard_map/all_to_all | solution.py:147
  127.0 1.4 %shard_map.59 = bf16[16,256,256]{2,1,0:T(8,128)(2,1)} custom-call(bf16[16,144,256]{2,1,0:T(8,128)(2,1)S(1)} %all-to-all-done.t_ref, bf16[256,256]{1,0:T(8,128)(2,1)S(1)} %bitcast.6, bf16[16,256,256]{2,1,0:T(8,128)(2,1)} %shard_map.58.rest_0_), custom_call_target="tpu_custom_call", output_to_operand_aliasing={{}: (2, {})} | custom-call | tf_op jit(solution)/shard_map/pallas_call | solution.py:115
  (6 shorter events, 0.0 us)
Async XLA Ops:
  6.5 84.5 %all-gather.2.cloned.1.call-start = ((), (), s32[]{:S(2)}) async-start(), calls=%async_computation.2 | async-start | bytes 2506752 | tf_op jit(solution)/shard_map/all_gather | solution.py:151
  6.5 0.9 copy-start.4
  53.1 16.3 %collective-permute-start = (bf16[32,112,128]{2,1,0:T(8,128)(2,1)S(1)}, bf16[32,112,128]{2,1,0:T(8,128)(2,1)S(1)}, u32[]{:S(2)}, u32[]{:S(2)}) collective-permute-start(bf16[32,112,128]{2,1,0:T(8,128)(2,1)S(1)} %all_gather.11.own_ref), channel_id=1, source_target_pairs={{0,16},{16,0},{1,17},{17,1},{2,18},{18,2},{3,19},{19,3},{4,20},{20... | collective-permute-start | bytes 2752520 | tf_op jit(solution)/shard_map/ppermute | solution.py:153
  69.4 0.9 copy-start.6
  70.3 1.6 %copy-start = (bf16[64,128,128]{2,1,0:T(8,128)(2,1)S(1)}, bf16[64,128,128]{2,1,0:T(8,128)(2,1)}, u32[]{:S(2)}) copy-start(bf16[64,128,128]{2,1,0:T(8,128)(2,1)} %param.6) | copy-start | bytes 6291460
  71.9 1.2 copy-start.7
  73.1 0.7 copy-start.8
  73.7 17.3 %copy-start.1 = (bf16[64,128,128]{2,1,0:T(8,128)(2,1)S(1)}, bf16[64,128,128]{2,1,0:T(8,128)(2,1)}, u32[]{:S(2)}) copy-start(bf16[64,128,128]{2,1,0:T(8,128)(2,1)} %param.6) | copy-start | bytes 6291460
  73.7 17.3 %copy-start.9 = (s32[1,16]{1,0:T(1,128)S(1)}, s32[1,16]{1,0:T(1,128)}, u32[]{:S(2)}) copy-start(s32[1,16]{1,0:T(1,128)} %owner_ref.3) | copy-start | bytes 196
  76.0 0.9 copy-start.2
  76.9 28.5 %all-to-all-start.1 = ((bf16[16,112,256]{2,1,0:T(8,128)(2,1)}), bf16[16,112,256]{2,1,0:T(8,128)(2,1)S(1)}, u32[]{:S(2)}, u32[]{:S(2)}) async-start(bf16[16,112,256]{2,1,0:T(8,128)(2,1)} %copy-done.2), calls=%async_computation.1 | async-start | bytes 1835008 | tf_op jit(solution)/shard_map/all_to_all | solution.py:147
  91.1 1.7 %copy-start.3 = (bf16[64,144,128]{2,1,0:T(8,128)(2,1)S(1)}, bf16[64,144,128]{2,1,0:T(8,128)(2,1)}, u32[]{:S(2)}) copy-start(bf16[64,144,128]{2,1,0:T(8,128)(2,1)} %all-gather.2.cloned.1.call-done.panels_ref) | copy-start | bytes 7077892
  96.0 13.7 %copy-start.5 = (bf16[2,128,256]{2,1,0:T(8,128)(2,1)S(1)}, bf16[2,128,256]{2,1,0:T(8,128)(2,1)}, u32[]{:S(2)}) copy-start(bf16[2,128,256]{2,1,0:T(8,128)(2,1)} %p_ref.1) | copy-start | bytes 393220
  105.5 21.6 %all-to-all-start = ((bf16[16,144,256]{2,1,0:T(8,128)(2,1)}), bf16[16,144,256]{2,1,0:T(8,128)(2,1)S(1)}, u32[]{:S(2)}, u32[]{:S(2)}) async-start(bf16[16,144,256]{2,1,0:T(8,128)(2,1)} %shard_map.56), calls=%async_computation | async-start | bytes 2359296 | tf_op jit(solution)/shard_map/all_to_all | solution.py:147
Sparse Core Ops, SparseCore 0:
  13.9 72.3 all-gather.1

commit v2 on v1

--- a/solution.py
+++ b/solution.py
@@ -11,12 +11,13 @@
 
 AXES = ("yl", "x", "core", "yh", "z")
 ROW, COL = AXES[:3], AXES[3:]
-EARLY = 112
-VMEM = 40 * 1024 * 1024
-
-
-def params():
-    return pltpu.CompilerParams(vmem_limit_bytes=VMEM)
+EARLY = 96
+SOME, MOST = 24 * 1024 * 1024, 58 * 1024 * 1024
+PARTS = 2
+
+
+def params(limit):
+    return pltpu.CompilerParams(vmem_limit_bytes=limit)
 
 
 def in_vmem():
@@ -46,51 +47,72 @@
         ),
         in_specs=[in_vmem()],
         out_specs=(in_vmem(), in_vmem()),
-        compiler_params=params(),
+        compiler_params=params(SOME),
     )(p)
 
 
-def terms(owner_ref, row_ref, count_ref, panel, a_ref, out_ref):
-    groups, _, width = out_ref.shape
-    block = a_ref.shape[2]
+def terms(fetches, panel, a_ref, a_held, out_ref, out_held, a_sems, out_sems):
+    groups, _, width = out_held.shape
+    block = a_held.shape[2]
     fine = width // block
-
-    def bucket(s, carry):
-        owner = owner_ref[0, s]
-        for g in range(fine):
-            count = count_ref[s, g]
-            slots = []
-            for m in range(2):
-                found = panel(owner, row_ref[s * fine + g, m])
-                slots.append(jnp.where(m < count, found, jnp.zeros_like(found)))
-            total = jnp.dot(
-                jnp.concatenate(slots, axis=1),
-                a_ref[s * fine + g],
-                preferred_element_type=jnp.float32,
-            )
-            out_ref[s, :, g * block : (g + 1) * block] = total.astype(out_ref.dtype)
-        return carry
-
-    lax.fori_loop(0, groups, bucket, 0, unroll=4)
-
-
-def early_kernel(side, owner_ref, row_ref, count_ref, here_ref, own_ref, other_ref, a_ref, out_ref):
-    fine = own_ref.shape[0] // side
-
-    def panel(owner, row):
-        at = (owner % side) * fine + row
-        return jnp.where(owner // side == here_ref[0], own_ref[at], other_ref[at])
-
-    terms(owner_ref, row_ref, count_ref, panel, a_ref, out_ref)
-
-
-def late_kernel(side, planes, owner_ref, row_ref, count_ref, panels_ref, a_ref, out_ref):
-    fine = panels_ref.shape[0] // (side * planes)
-
-    def panel(owner, row):
-        return panels_ref[((owner % side) * planes + owner // side) * fine + row]
-
-    terms(owner_ref, row_ref, count_ref, panel, a_ref, out_ref)
+    step = groups // PARTS
+    reads = [
+        pltpu.make_async_copy(
+            a_ref.at[pl.ds(part * step * fine, step * fine)],
+            a_held.at[pl.ds(part * step * fine, step * fine)],
+            a_sems.at[part],
+        )
+        for part in range(PARTS)
+    ]
+    for copy in fetches + reads:
+        copy.start()
+    for copy in fetches:
+        copy.wait()
+    writes = []
+    for part in range(PARTS):
+        reads[part].wait()
+        for s in range(part * step, (part + 1) * step):
+            for g in range(fine):
+                slots = [panel((s * fine + g) * 2 + m) for m in range(2)]
+                total = jnp.dot(
+                    jnp.concatenate(slots, axis=1),
+                    a_held[s * fine + g],
+                    preferred_element_type=jnp.float32,
+                )
+                out_held[s, :, g * block : (g + 1) * block] = total.astype(out_held.dtype)
+        span = pl.ds(part * step, step)
+        writes.append(pltpu.make_async_copy(out_held.at[span], out_ref.at[span], out_sems.at[part]))
+        writes[-1].start()
+    for copy in writes:
+        copy.wait()
+
+
+def early_kernel(planes, fine, table_ref, own_ref, other_ref, a_ref, out_ref, held, a_held, out_held, sems, a_sems, out_sems):
+    slots = table_ref.shape[0] - 1
+    here = table_ref[slots]
+
+    def panel(slot):
+        at = table_ref[slot]
+        live = at >= 0
+        at = jnp.maximum(at, 0)
+        away = jnp.where((at // fine) % planes == here, 0, 1)
+        found = held[away, at // (fine * planes) * fine + at % fine]
+        return jnp.where(live, found, jnp.zeros_like(found))
+
+    fetches = [
+        pltpu.make_async_copy(ref, held.at[i], sems.at[i]) for i, ref in enumerate((own_ref, other_ref))
+    ]
+    terms(fetches, panel, a_ref, a_held, out_ref, out_held, a_sems, out_sems)
+
+
+def late_kernel(table_ref, panels_ref, a_ref, out_ref, held, a_held, out_held, sems, a_sems, out_sems):
+    def panel(slot):
+        at = table_ref[slot]
+        found = held[jnp.maximum(at, 0)]
+        return jnp.where(at >= 0, found, jnp.zeros_like(found))
+
+    fetches = [pltpu.make_async_copy(panels_ref, held, sems.at[0])]
+    terms(fetches, panel, a_ref, a_held, out_ref, out_held, a_sems, out_sems)
 
 
 def final_kernel(first, t_ref, p_ref, *rest):
@@ -122,7 +144,7 @@
             pltpu.SemaphoreType.DMA((groups,)),
         ],
         input_output_aliases={2: 0} if more else {},
-        compiler_params=params(),
+        compiler_params=params(SOME),
     )(arrived, p, *more)
 
 
@@ -135,15 +157,22 @@
     flat = p.reshape(fine * block, width)
     early, late = split_panels(p)
 
-    def sent(kernel, rows, operands):
-        specs = [in_smem()] * 3 + [in_smem() if x.ndim == 1 else in_vmem() for x in operands]
+    def sent(kernel, rows, held, panels):
         summed = pl.pallas_call(
             kernel,
             out_shape=jax.ShapeDtypeStruct((groups, rows, fine * block), p.dtype),
-            in_specs=specs + [in_vmem()],
-            out_specs=in_vmem(),
-            compiler_params=params(),
-        )(owner, row, count, *operands, stacked)
+            in_specs=[in_smem()] + [pl.BlockSpec(memory_space=pl.ANY)] * (len(panels) + 1),
+            out_specs=pl.BlockSpec(memory_space=pl.ANY),
+            scratch_shapes=[
+                pltpu.VMEM(held, p.dtype),
+                pltpu.VMEM(stacked.shape, p.dtype),
+                pltpu.VMEM((groups, rows, fine * block), p.dtype),
+                pltpu.SemaphoreType.DMA((len(panels),)),
+                pltpu.SemaphoreType.DMA((PARTS,)),
+                pltpu.SemaphoreType.DMA((PARTS,)),
+            ],
+            compiler_params=params(MOST),
+        )(table, *panels, stacked)
         return lax.all_to_all(summed, ROW, split_axis=0, concat_axis=0, tiled=True)
 
     pair = lax.all_gather(late, "yh", axis=0, tiled=True)
@@ -151,10 +180,16 @@
     late_panels = lax.all_gather(pair, "z", axis=0, tiled=True)
     own = lax.all_gather(early, "z", axis=0, tiled=True)
     other = lax.ppermute(own, "yh", [(0, 1), (1, 0)])
+
+    at = (owner % side) * planes + owner // side
+    at = at.reshape(groups, 1, 1) * fine + row.reshape(groups, fine, -1)
+    live = jnp.arange(at.shape[2], dtype=jnp.int32)[None, None] < count[:, :, None]
     here = lax.axis_index("yh").astype(jnp.int32).reshape(1)
-    arrived = sent(functools.partial(early_kernel, side), EARLY, (here, own, other))
+    table = jnp.concatenate([jnp.where(live, at, -1).reshape(-1), here])
+
+    arrived = sent(functools.partial(early_kernel, planes, fine), EARLY, (planes, *own.shape), (own, other))
     result = final(0, arrived, flat)
-    arrived = sent(functools.partial(late_kernel, side, planes), width - EARLY, (late_panels,))
+    arrived = sent(late_kernel, width - EARLY, late_panels.shape, (late_panels,))
     return final(EARLY, arrived, flat, result)
 
 

time: 136 us -> 134 us (0.985)
  local copies, waits for them, and re-layouts: 9.35 us -> 3.74 us
  starting transfers between devices: 21.9 us -> 26.7 us
  waiting for transfers between devices: 36.7 us -> 33 us
  Pallas kernels: 8.22 us -> 11.6 us
  blocking collectives: 45.5 us -> 43.1 us
  other arithmetic: 0 us -> 1.43 us
    unnamed x22 -> x10, local copies, waits for them, and re-layouts: 9.35 us -> 3.32 us
    ppermute x1, waiting for transfers between devices: 11.1 us -> 7.21 us  [on_device(): other = lax.ppermute(own, 'yh', [(0, 1), (1, 0)])]
    all_gather x1, waiting for transfers between devices: 0.01 us -> 3.49 us  [on_device(): late_panels = lax.all_gather(pair, 'z', axis=0, tiled=True)]
    pallas_call x2, Pallas kernels: 5.53 us -> 8.89 us  [sent(): pl.pallas_call(kernel, out_shape=jax.ShapeDtypeStruct((groups, rows, fine...]
    all_to_all x2, waiting for transfers between devices: 25.6 us -> 22.3 us  [sent(): return lax.all_to_all(summed, ROW, split_axis=0, concat_axis=0, tiled=True)]
    all_to_all x2, starting transfers between devices: 18.3 us -> 21.6 us  [sent(): return lax.all_to_all(summed, ROW, split_axis=0, concat_axis=0, tiled=True)]
    all_gather x1, blocking collectives: 39.3 us -> 36.8 us  [on_device(): own = lax.all_gather(early, 'z', axis=0, tiled=True)]
    ppermute x1, starting transfers between devices: 3.63 us -> 5.16 us  [on_device(): other = lax.ppermute(own, 'yh', [(0, 1), (1, 0)])]
  transfers between devices with their start and end apart: 4 -> 4, of which waited for: 3 -> 4; matrix products, arithmetic and copies ran while one was open for 1% -> 3% of each run, Pallas kernels for 5% -> 8%
where the time goes in v2:
time: 134 us; the launch traced here: 133 us
  blocking collectives  43.1 us (32%)
  waiting for transfers between devices  33 us (25%)
  starting transfers between devices  26.7 us (20%)
  between operations  13.5 us (10%)
  Pallas kernels  11.6 us (9%)
  local copies, waits for them, and re-layouts  3.74 us (3%)
  other arithmetic  1.43 us (1%)
    all_gather x1, blocking collectives, on_device(): own = lax.all_gather(early, 'z', axis=0, tiled=True)  36.8 us
    all_to_all x2, waiting for transfers between devices, sent(): return lax.all_to_all(summed, ROW, split_axis=0, concat_axis=0, tiled=True)  22.3 us
    all_to_all x2, starting transfers between devices, sent(): return lax.all_to_all(summed, ROW, split_axis=0, concat_axis=0, tiled=True)  21.6 us
    pallas_call x2, Pallas kernels, sent(): pl.pallas_call(kernel, out_shape=jax.ShapeDtypeStruct((groups, rows, fine...  8.89 us
    ppermute x1, waiting for transfers between devices, on_device(): other = lax.ppermute(own, 'yh', [(0, 1), (1, 0)])  7.21 us
    all_gather x1, blocking collectives, on_device(): pair = lax.all_gather(late, 'yh', axis=0, tiled=True)  6.33 us
    ppermute x1, starting transfers between devices, on_device(): other = lax.ppermute(own, 'yh', [(0, 1), (1, 0)])  5.16 us
    all_gather x1, waiting for transfers between devices, on_device(): late_panels = lax.all_gather(pair, 'z', axis=0, tiled=True)  3.49 us
  transfers between devices with their start and end apart: 4, of which 4 were waited for; matrix products, arithmetic and copies ran while one was open for 3% of the time, Pallas kernels for 8%

profile of v2, /device:TPU:1, one launch (start us, length us, event | category | flops | bytes accessed | tf_op | source)
XLA Modules:
  0.0 133.1 jit_solution(5930224712797265268)
XLA Ops:
  6.5 0.0 all-gather.2.cloned.1.call-start
  6.5 0.0 copy-start
  6.5 0.9 copy-done
  7.4 0.1 shard_map.55
  7.5 6.3 %all_gather.9 = bf16[4,160,128]{2,1,0:T(8,128)(2,1)} all-gather(bf16[2,160,128]{2,1,0:T(8,128)(2,1)S(1)} %get-tuple-element.10), channel_id=1, replica_groups=mesh['yl'=2,'x'=4,'core'=2,'yh'=2,'z'=16] {'yh'}, dimensions={0}, use_global_device_ids=true | all-gather | bytes 245760 | tf_op jit(solution)/shard_map/all_gather | solution.py:178
  13.9 0.0 all-gather.2.cloned.1.call-update
  13.9 36.8 %all_gather.11.own_ref = bf16[32,96,128]{2,1,0:T(8,128)(2,1)S(1)} all-gather(bf16[2,96,128]{2,1,0:T(8,128)(2,1)S(1)} %get-tuple-element.12), channel_id=1, replica_groups=mesh['yl'=2,'x'=4,'core'=2,'yh'=2,'z'=16] {'z'}, dimensions={0}, use_global_device_ids=true | all-gather | bytes 835584 | tf_op jit(solution)/shard_map/all_gather | solution.py:181
  50.7 0.0 copy-start.2
  50.7 5.2 %collective-permute-start = (bf16[32,96,128]{2,1,0:T(8,128)(2,1)S(1)}, bf16[32,96,128]{2,1,0:T(8,128)(2,1)S(1)}, u32[]{:S(2)}, u32[]{:S(2)}) collective-permute-start(bf16[32,96,128]{2,1,0:T(8,128)(2,1)S(1)} %all_gather.11.own_ref), channel_id=1, source_target_pairs={{0,16},{16,0},{1,17},{17,1},{2,18},{18,2},{3,19},{19,3},{4,20},{20... | collective-permute-start | bytes 2359304 | tf_op jit(solution)/shard_map/ppermute | solution.py:182
  55.9 0.8 copy.11
  56.6 0.1 iota_compare_fusion
  56.7 0.1 lt.26
  56.8 0.7 multiply_bitcast_fusion
  57.5 0.1 add.23
  57.6 0.1 add.24
  57.7 0.8 copy.12
  58.5 0.1 reshape.29
  58.6 0.7 pad_add_fusion.table_ref
  59.3 7.2 %collective-permute-done.other_ref = bf16[32,96,128]{2,1,0:T(8,128)(2,1)S(1)} collective-permute-done((bf16[32,96,128]{2,1,0:T(8,128)(2,1)S(1)}, bf16[32,96,128]{2,1,0:T(8,128)(2,1)S(1)}, u32[]{:S(2)}, u32[]{:S(2)}) %collective-permute-start) | collective-permute-done | bytes 786464 | tf_op jit(solution)/shard_map/ppermute | solution.py:182
  66.5 0.0 copy-done.2
  66.5 0.9 copy-done.3
  67.4 4.3 %shard_map.57 = bf16[16,96,256]{2,1,0:T(8,128)(2,1)} custom-call(s32[65]{0:T(128)} %pad_add_fusion.table_ref, bf16[32,96,128]{2,1,0:T(8,128)(2,1)} %copy-done.2, bf16[32,96,128]{2,1,0:T(8,128)(2,1)} %copy-done.3, bf16[32,256,128]{2,1,0:T(8,128)(2,1)} %bitcast.7), custom_call_target="tpu_custom_call" | custom-call | tf_op jit(solution)/shard_map/pallas_call | solution.py:161
  71.6 12.9 %all-to-all-start.1 = ((bf16[16,96,256]{2,1,0:T(8,128)(2,1)}), bf16[16,96,256]{2,1,0:T(8,128)(2,1)S(1)}, u32[]{:S(2)}, u32[]{:S(2)}) async-start(bf16[16,96,256]{2,1,0:T(8,128)(2,1)} %shard_map.57), calls=%async_computation.1 | async-start | bytes 1572864 | tf_op jit(solution)/shard_map/all_to_all | solution.py:176
  84.5 3.5 %all-gather.2.cloned.1.call-done.panels_ref = bf16[64,160,128]{2,1,0:T(8,128)(2,1)} async-done(((bf16[4,160,128]{2,1,0:T(8,128)(2,1)}), bf16[64,160,128]{2,1,0:T(8,128)(2,1)}) %all-gather.2.cloned.1.call-update) | async-done | bytes 2621456 | tf_op jit(solution)/shard_map/all_gather | solution.py:180
  88.0 4.6 %shard_map.56 = bf16[16,160,256]{2,1,0:T(8,128)(2,1)} custom-call(s32[65]{0:T(128)} %pad_add_fusion.table_ref, bf16[64,160,128]{2,1,0:T(8,128)(2,1)} %all-gather.2.cloned.1.call-done.panels_ref, bf16[32,256,128]{2,1,0:T(8,128)(2,1)} %bitcast.8), custom_call_target="tpu_custom_call" | custom-call | tf_op jit(solution)/shard_map/pallas_call | solution.py:161
  92.7 0.0 copy-start.1
  92.7 4.9 %all-to-all-done.1.t_ref = bf16[16,96,256]{2,1,0:T(8,128)(2,1)S(1)} async-done(((bf16[16,96,256]{2,1,0:T(8,128)(2,1)}), bf16[16,96,256]{2,1,0:T(8,128)(2,1)S(1)}, u32[]{:S(2)}, u32[]{:S(2)}) %all-to-all-start.1) | async-done | bytes 786464 | tf_op jit(solution)/shard_map/all_to_all | solution.py:176
  97.5 8.7 %all-to-all-start = ((bf16[16,160,256]{2,1,0:T(8,128)(2,1)}), bf16[16,160,256]{2,1,0:T(8,128)(2,1)S(1)}, u32[]{:S(2)}, u32[]{:S(2)}) async-start(bf16[16,160,256]{2,1,0:T(8,128)(2,1)} %shard_map.56), calls=%async_computation | async-start | bytes 2621440 | tf_op jit(solution)/shard_map/all_to_all | solution.py:176
  106.2 0.0 copy-done.1
  106.2 1.3 shard_map.58.rest_0_
  107.5 17.4 %all-to-all-done.t_ref = bf16[16,160,256]{2,1,0:T(8,128)(2,1)S(1)} async-done(((bf16[16,160,256]{2,1,0:T(8,128)(2,1)}), bf16[16,160,256]{2,1,0:T(8,128)(2,1)S(1)}, u32[]{:S(2)}, u32[]{:S(2)}) %all-to-all-start) | async-done | bytes 1310752 | tf_op jit(solution)/shard_map/all_to_all | solution.py:176
  124.9 1.4 %shard_map.59 = bf16[16,256,256]{2,1,0:T(8,128)(2,1)} custom-call(bf16[16,160,256]{2,1,0:T(8,128)(2,1)S(1)} %all-to-all-done.t_ref, bf16[256,256]{1,0:T(8,128)(2,1)S(1)} %bitcast.6, bf16[16,256,256]{2,1,0:T(8,128)(2,1)} %shard_map.58.rest_0_), custom_call_target="tpu_custom_call", output_to_operand_aliasing={{}: (2, {})} | custom-call | tf_op jit(solution)/shard_map/pallas_call | solution.py:137
  (2 shorter events, 0.0 us)
Async XLA Ops:
  6.5 81.5 %all-gather.2.cloned.1.call-start = ((), (), s32[]{:S(2)}) async-start(), calls=%async_computation.2 | async-start | bytes 2785280 | tf_op jit(solution)/shard_map/all_gather | solution.py:180
  6.5 0.9 copy-start
  50.7 15.8 %copy-start.2 = (bf16[32,96,128]{2,1,0:T(8,128)(2,1)}, bf16[32,96,128]{2,1,0:T(8,128)(2,1)S(1)}, u32[]{:S(2)}) copy-start(bf16[32,96,128]{2,1,0:T(8,128)(2,1)S(1)} %all_gather.11.own_ref) | copy-start | bytes 2359300
  50.7 15.8 %collective-permute-start = (bf16[32,96,128]{2,1,0:T(8,128)(2,1)S(1)}, bf16[32,96,128]{2,1,0:T(8,128)(2,1)S(1)}, u32[]{:S(2)}, u32[]{:S(2)}) collective-permute-start(bf16[32,96,128]{2,1,0:T(8,128)(2,1)S(1)} %all_gather.11.own_ref), channel_id=1, source_target_pairs={{0,16},{16,0},{1,17},{17,1},{2,18},{18,2},{3,19},{19,3},{4,20},{20... | collective-permute-start | bytes 2359304 | tf_op jit(solution)/shard_map/ppermute | solution.py:182
  66.5 0.9 copy-start.3
  71.6 25.9 %all-to-all-start.1 = ((bf16[16,96,256]{2,1,0:T(8,128)(2,1)}), bf16[16,96,256]{2,1,0:T(8,128)(2,1)S(1)}, u32[]{:S(2)}, u32[]{:S(2)}) async-start(bf16[16,96,256]{2,1,0:T(8,128)(2,1)} %shard_map.57), calls=%async_computation.1 | async-start | bytes 1572864 | tf_op jit(solution)/shard_map/all_to_all | solution.py:176
  92.7 13.6 %copy-start.1 = (bf16[2,128,256]{2,1,0:T(8,128)(2,1)S(1)}, bf16[2,128,256]{2,1,0:T(8,128)(2,1)}, u32[]{:S(2)}) copy-start(bf16[2,128,256]{2,1,0:T(8,128)(2,1)} %p_ref.1) | copy-start | bytes 393220
  97.5 27.3 %all-to-all-start = ((bf16[16,160,256]{2,1,0:T(8,128)(2,1)}), bf16[16,160,256]{2,1,0:T(8,128)(2,1)S(1)}, u32[]{:S(2)}, u32[]{:S(2)}) async-start(bf16[16,160,256]{2,1,0:T(8,128)(2,1)} %shard_map.56), calls=%async_computation | async-start | bytes 2621440 | tf_op jit(solution)/shard_map/all_to_all | solution.py:176
Sparse Core Ops, SparseCore 0:
  14.0 73.9 all-gather.1

commit v3 on v2

--- a/solution.py
+++ b/solution.py
@@ -22,10 +22,6 @@
 
 def in_vmem():
     return pl.BlockSpec(memory_space=pltpu.VMEM)
-
-
-def in_smem():
-    return pl.BlockSpec(memory_space=pltpu.SMEM)
 
 
 def split_kernel(p_ref, early_ref, late_ref):
@@ -51,7 +47,7 @@
     )(p)
 
 
-def terms(fetches, panel, a_ref, a_held, out_ref, out_held, a_sems, out_sems):
+def terms(fetches, table_fetch, panel, a_ref, a_held, out_ref, out_held, a_sems, out_sems):
     groups, _, width = out_held.shape
     block = a_held.shape[2]
     fine = width // block
@@ -64,9 +60,9 @@
         )
         for part in range(PARTS)
     ]
-    for copy in fetches + reads:
+    for copy in fetches + reads + [table_fetch]:
         copy.start()
-    for copy in fetches:
+    for copy in [table_fetch] + fetches:
         copy.wait()
     writes = []
     for part in range(PARTS):
@@ -87,32 +83,33 @@
         copy.wait()
 
 
-def early_kernel(planes, fine, table_ref, own_ref, other_ref, a_ref, out_ref, held, a_held, out_held, sems, a_sems, out_sems):
+def early_kernel(planes, fine, table_ref, own_ref, other_ref, a_ref, out_ref, held, a_held, out_held, table, table_sem, sems, a_sems, out_sems):
     slots = table_ref.shape[0] - 1
-    here = table_ref[slots]
 
     def panel(slot):
-        at = table_ref[slot]
+        at = table[slot]
         live = at >= 0
         at = jnp.maximum(at, 0)
-        away = jnp.where((at // fine) % planes == here, 0, 1)
+        away = jnp.where((at // fine) % planes == table[slots], 0, 1)
         found = held[away, at // (fine * planes) * fine + at % fine]
         return jnp.where(live, found, jnp.zeros_like(found))
 
     fetches = [
         pltpu.make_async_copy(ref, held.at[i], sems.at[i]) for i, ref in enumerate((own_ref, other_ref))
     ]
-    terms(fetches, panel, a_ref, a_held, out_ref, out_held, a_sems, out_sems)
-
-
-def late_kernel(table_ref, panels_ref, a_ref, out_ref, held, a_held, out_held, sems, a_sems, out_sems):
+    table_fetch = pltpu.make_async_copy(table_ref, table, table_sem)
+    terms(fetches, table_fetch, panel, a_ref, a_held, out_ref, out_held, a_sems, out_sems)
+
+
+def late_kernel(table_ref, panels_ref, a_ref, out_ref, held, a_held, out_held, table, table_sem, sems, a_sems, out_sems):
     def panel(slot):
-        at = table_ref[slot]
+        at = table[slot]
         found = held[jnp.maximum(at, 0)]
         return jnp.where(at >= 0, found, jnp.zeros_like(found))
 
     fetches = [pltpu.make_async_copy(panels_ref, held, sems.at[0])]
-    terms(fetches, panel, a_ref, a_held, out_ref, out_held, a_sems, out_sems)
+    table_fetch = pltpu.make_async_copy(table_ref, table, table_sem)
+    terms(fetches, table_fetch, panel, a_ref, a_held, out_ref, out_held, a_sems, out_sems)
 
 
 def final_kernel(first, t_ref, p_ref, *rest):
@@ -161,12 +158,14 @@
         summed = pl.pallas_call(
             kernel,
             out_shape=jax.ShapeDtypeStruct((groups, rows, fine * block), p.dtype),
-            in_specs=[in_smem()] + [pl.BlockSpec(memory_space=pl.ANY)] * (len(panels) + 1),
+            in_specs=[pl.BlockSpec(memory_space=pl.ANY)] * (len(panels) + 2),
             out_specs=pl.BlockSpec(memory_space=pl.ANY),
             scratch_shapes=[
                 pltpu.VMEM(held, p.dtype),
                 pltpu.VMEM(stacked.shape, p.dtype),
                 pltpu.VMEM((groups, rows, fine * block), p.dtype),
+                pltpu.SMEM(table.shape, table.dtype),
+                pltpu.SemaphoreType.DMA,
                 pltpu.SemaphoreType.DMA((len(panels),)),
                 pltpu.SemaphoreType.DMA((PARTS,)),
                 pltpu.SemaphoreType.DMA((PARTS,)),

time: 134 us -> 133 us (level)
  transfers between devices with their start and end apart: 4 -> 4, of which waited for: 4 -> 4; matrix products, arithmetic and copies ran while one was open for 3% -> 3% of each run, Pallas kernels for 8% -> 7%
where the time goes in v3:
time: 133 us; the launch traced here: 132 us
  blocking collectives  43.1 us (32%)
  waiting for transfers between devices  33.6 us (25%)
  starting transfers between devices  26.7 us (20%)
  between operations  13.5 us (10%)
  Pallas kernels  10.3 us (8%)
  local copies, waits for them, and re-layouts  3.74 us (3%)
  other arithmetic  1.43 us (1%)
    all_gather x1, blocking collectives, on_device(): own = lax.all_gather(early, 'z', axis=0, tiled=True)  36.8 us
    all_to_all x2, waiting for transfers between devices, sent(): return lax.all_to_all(summed, ROW, split_axis=0, concat_axis=0, tiled=True)  22.3 us
    all_to_all x2, starting transfers between devices, sent(): return lax.all_to_all(summed, ROW, split_axis=0, concat_axis=0, tiled=True)  21.6 us
    pallas_call x2, Pallas kernels, sent(): pl.pallas_call(kernel, out_shape=jax.ShapeDtypeStruct((groups, rows, fine...  7.58 us
    ppermute x1, waiting for transfers between devices, on_device(): other = lax.ppermute(own, 'yh', [(0, 1), (1, 0)])  7.21 us
    all_gather x1, blocking collectives, on_device(): pair = lax.all_gather(late, 'yh', axis=0, tiled=True)  6.33 us
    ppermute x1, starting transfers between devices, on_device(): other = lax.ppermute(own, 'yh', [(0, 1), (1, 0)])  5.16 us
    all_gather x1, waiting for transfers between devices, on_device(): late_panels = lax.all_gather(pair, 'z', axis=0, tiled=True)  4.14 us
  transfers between devices with their start and end apart: 4, of which 4 were waited for; matrix products, arithmetic and copies ran while one was open for 3% of the time, Pallas kernels for 7%

profile of v3, /device:TPU:1, one launch (start us, length us, event | category | flops | bytes accessed | tf_op | source)
XLA Modules:
  0.0 132.5 jit_solution(4977256616418058652)
XLA Ops:
  6.5 0.0 all-gather.2.cloned.1.call-start
  6.5 0.0 copy-start
  6.5 0.9 copy-done
  7.4 0.1 shard_map.55
  7.5 6.3 %all_gather.9 = bf16[4,160,128]{2,1,0:T(8,128)(2,1)} all-gather(bf16[2,160,128]{2,1,0:T(8,128)(2,1)S(1)} %get-tuple-element.10), channel_id=1, replica_groups=mesh['yl'=2,'x'=4,'core'=2,'yh'=2,'z'=16] {'yh'}, dimensions={0}, use_global_device_ids=true | all-gather | bytes 245760 | tf_op jit(solution)/shard_map/all_gather | solution.py:177
  13.9 0.0 all-gather.2.cloned.1.call-update
  13.9 36.8 %all_gather.11.own_ref = bf16[32,96,128]{2,1,0:T(8,128)(2,1)S(1)} all-gather(bf16[2,96,128]{2,1,0:T(8,128)(2,1)S(1)} %get-tuple-element.12), channel_id=1, replica_groups=mesh['yl'=2,'x'=4,'core'=2,'yh'=2,'z'=16] {'z'}, dimensions={0}, use_global_device_ids=true | all-gather | bytes 835584 | tf_op jit(solution)/shard_map/all_gather | solution.py:180
  50.7 0.0 copy-start.2
  50.7 5.2 %collective-permute-start = (bf16[32,96,128]{2,1,0:T(8,128)(2,1)S(1)}, bf16[32,96,128]{2,1,0:T(8,128)(2,1)S(1)}, u32[]{:S(2)}, u32[]{:S(2)}) collective-permute-start(bf16[32,96,128]{2,1,0:T(8,128)(2,1)S(1)} %all_gather.11.own_ref), channel_id=1, source_target_pairs={{0,16},{16,0},{1,17},{17,1},{2,18},{18,2},{3,19},{19,3},{4,20},{20... | collective-permute-start | bytes 2359304 | tf_op jit(solution)/shard_map/ppermute | solution.py:181
  55.9 0.8 copy.11
  56.6 0.1 iota_compare_fusion
  56.7 0.1 lt.26
  56.8 0.7 multiply_bitcast_fusion
  57.5 0.1 add.23
  57.6 0.1 add.24
  57.7 0.8 copy.12
  58.5 0.1 reshape.29
  58.6 0.7 pad_add_fusion.table_ref
  59.3 7.2 %collective-permute-done.other_ref = bf16[32,96,128]{2,1,0:T(8,128)(2,1)S(1)} collective-permute-done((bf16[32,96,128]{2,1,0:T(8,128)(2,1)S(1)}, bf16[32,96,128]{2,1,0:T(8,128)(2,1)S(1)}, u32[]{:S(2)}, u32[]{:S(2)}) %collective-permute-start) | collective-permute-done | bytes 786464 | tf_op jit(solution)/shard_map/ppermute | solution.py:181
  66.5 0.0 copy-done.2
  66.5 0.9 copy-done.3
  67.4 3.6 %shard_map.57 = bf16[16,96,256]{2,1,0:T(8,128)(2,1)} custom-call(s32[65]{0:T(128)} %pad_add_fusion.table_ref, bf16[32,96,128]{2,1,0:T(8,128)(2,1)} %copy-done.2, bf16[32,96,128]{2,1,0:T(8,128)(2,1)} %copy-done.3, bf16[32,256,128]{2,1,0:T(8,128)(2,1)} %bitcast.7), custom_call_target="tpu_custom_call" | custom-call | tf_op jit(solution)/shard_map/pallas_call | solution.py:158
  71.0 12.9 %all-to-all-start.1 = ((bf16[16,96,256]{2,1,0:T(8,128)(2,1)}), bf16[16,96,256]{2,1,0:T(8,128)(2,1)S(1)}, u32[]{:S(2)}, u32[]{:S(2)}) async-start(bf16[16,96,256]{2,1,0:T(8,128)(2,1)} %shard_map.57), calls=%async_computation.1 | async-start | bytes 1572864 | tf_op jit(solution)/shard_map/all_to_all | solution.py:175
  83.9 4.1 %all-gather.2.cloned.1.call-done.panels_ref = bf16[64,160,128]{2,1,0:T(8,128)(2,1)} async-done(((bf16[4,160,128]{2,1,0:T(8,128)(2,1)}), bf16[64,160,128]{2,1,0:T(8,128)(2,1)}) %all-gather.2.cloned.1.call-update) | async-done | bytes 2621456 | tf_op jit(solution)/shard_map/all_gather | solution.py:179
  88.0 4.0 %shard_map.56 = bf16[16,160,256]{2,1,0:T(8,128)(2,1)} custom-call(s32[65]{0:T(128)} %pad_add_fusion.table_ref, bf16[64,160,128]{2,1,0:T(8,128)(2,1)} %all-gather.2.cloned.1.call-done.panels_ref, bf16[32,256,128]{2,1,0:T(8,128)(2,1)} %bitcast.8), custom_call_target="tpu_custom_call" | custom-call | tf_op jit(solution)/shard_map/pallas_call | solution.py:158
  92.0 0.0 copy-start.1
  92.0 4.9 %all-to-all-done.1.t_ref = bf16[16,96,256]{2,1,0:T(8,128)(2,1)S(1)} async-done(((bf16[16,96,256]{2,1,0:T(8,128)(2,1)}), bf16[16,96,256]{2,1,0:T(8,128)(2,1)S(1)}, u32[]{:S(2)}, u32[]{:S(2)}) %all-to-all-start.1) | async-done | bytes 786464 | tf_op jit(solution)/shard_map/all_to_all | solution.py:175
  96.9 8.7 %all-to-all-start = ((bf16[16,160,256]{2,1,0:T(8,128)(2,1)}), bf16[16,160,256]{2,1,0:T(8,128)(2,1)S(1)}, u32[]{:S(2)}, u32[]{:S(2)}) async-start(bf16[16,160,256]{2,1,0:T(8,128)(2,1)} %shard_map.56), calls=%async_computation | async-start | bytes 2621440 | tf_op jit(solution)/shard_map/all_to_all | solution.py:175
  105.6 0.0 copy-done.1
  105.6 1.3 shard_map.58.rest_0_
  106.8 17.4 %all-to-all-done.t_ref = bf16[16,160,256]{2,1,0:T(8,128)(2,1)S(1)} async-done(((bf16[16,160,256]{2,1,0:T(8,128)(2,1)}), bf16[16,160,256]{2,1,0:T(8,128)(2,1)S(1)}, u32[]{:S(2)}, u32[]{:S(2)}) %all-to-all-start) | async-done | bytes 1310752 | tf_op jit(solution)/shard_map/all_to_all | solution.py:175
  124.2 1.4 %shard_map.59 = bf16[16,256,256]{2,1,0:T(8,128)(2,1)} custom-call(bf16[16,160,256]{2,1,0:T(8,128)(2,1)S(1)} %all-to-all-done.t_ref, bf16[256,256]{1,0:T(8,128)(2,1)S(1)} %bitcast.6, bf16[16,256,256]{2,1,0:T(8,128)(2,1)} %shard_map.58.rest_0_), custom_call_target="tpu_custom_call", output_to_operand_aliasing={{}: (2, {})} | custom-call | tf_op jit(solution)/shard_map/pallas_call | solution.py:134
  (2 shorter events, 0.0 us)
Async XLA Ops:
  6.5 81.5 %all-gather.2.cloned.1.call-start = ((), (), s32[]{:S(2)}) async-start(), calls=%async_computation.2 | async-start | bytes 2785280 | tf_op jit(solution)/shard_map/all_gather | solution.py:179
  6.5 0.9 copy-start
  50.7 15.8 %copy-start.2 = (bf16[32,96,128]{2,1,0:T(8,128)(2,1)}, bf16[32,96,128]{2,1,0:T(8,128)(2,1)S(1)}, u32[]{:S(2)}) copy-start(bf16[32,96,128]{2,1,0:T(8,128)(2,1)S(1)} %all_gather.11.own_ref) | copy-start | bytes 2359300
  50.7 15.8 %collective-permute-start = (bf16[32,96,128]{2,1,0:T(8,128)(2,1)S(1)}, bf16[32,96,128]{2,1,0:T(8,128)(2,1)S(1)}, u32[]{:S(2)}, u32[]{:S(2)}) collective-permute-start(bf16[32,96,128]{2,1,0:T(8,128)(2,1)S(1)} %all_gather.11.own_ref), channel_id=1, source_target_pairs={{0,16},{16,0},{1,17},{17,1},{2,18},{18,2},{3,19},{19,3},{4,20},{20... | collective-permute-start | bytes 2359304 | tf_op jit(solution)/shard_map/ppermute | solution.py:181
  66.5 0.9 copy-start.3
  71.0 25.9 %all-to-all-start.1 = ((bf16[16,96,256]{2,1,0:T(8,128)(2,1)}), bf16[16,96,256]{2,1,0:T(8,128)(2,1)S(1)}, u32[]{:S(2)}, u32[]{:S(2)}) async-start(bf16[16,96,256]{2,1,0:T(8,128)(2,1)} %shard_map.57), calls=%async_computation.1 | async-start | bytes 1572864 | tf_op jit(solution)/shard_map/all_to_all | solution.py:175
  92.0 13.6 %copy-start.1 = (bf16[2,128,256]{2,1,0:T(8,128)(2,1)S(1)}, bf16[2,128,256]{2,1,0:T(8,128)(2,1)}, u32[]{:S(2)}) copy-start(bf16[2,128,256]{2,1,0:T(8,128)(2,1)} %p_ref.1) | copy-start | bytes 393220
  96.9 27.3 %all-to-all-start = ((bf16[16,160,256]{2,1,0:T(8,128)(2,1)}), bf16[16,160,256]{2,1,0:T(8,128)(2,1)S(1)}, u32[]{:S(2)}, u32[]{:S(2)}) async-start(bf16[16,160,256]{2,1,0:T(8,128)(2,1)} %shard_map.56), calls=%async_computation | async-start | bytes 2621440 | tf_op jit(solution)/shard_map/all_to_all | solution.py:175
Sparse Core Ops, SparseCore 0:
  14.0 73.9 all-gather.1

commit v4 on v3

--- a/solution.py
+++ b/solution.py
@@ -11,7 +11,7 @@
 
 AXES = ("yl", "x", "core", "yh", "z")
 ROW, COL = AXES[:3], AXES[3:]
-EARLY = 96
+EARLY = 112
 SOME, MOST = 24 * 1024 * 1024, 58 * 1024 * 1024
 PARTS = 2
 
@@ -176,11 +176,12 @@
 
     pair = lax.all_gather(late, "yh", axis=0, tiled=True)
     early, pair = lax.optimization_barrier((early, pair))
-    late_panels = lax.all_gather(pair, "z", axis=0, tiled=True)
-    own = lax.all_gather(early, "z", axis=0, tiled=True)
+    down = [list(range(side - 1, -1, -1))]
+    late_panels = lax.all_gather(pair, "z", axis=0, tiled=True, axis_index_groups=down)
+    own = lax.all_gather(early, "z", axis=0, tiled=True, axis_index_groups=down)
     other = lax.ppermute(own, "yh", [(0, 1), (1, 0)])
 
-    at = (owner % side) * planes + owner // side
+    at = (side - 1 - owner % side) * planes + owner // side
     at = at.reshape(groups, 1, 1) * fine + row.reshape(groups, fine, -1)
     live = jnp.arange(at.shape[2], dtype=jnp.int32)[None, None] < count[:, :, None]
     here = lax.axis_index("yh").astype(jnp.int32).reshape(1)

time: 133 us -> 131 us (0.985)
  starting transfers between devices: 26.7 us -> 20.2 us
  waiting for transfers between devices: 33.6 us -> 37.2 us
    all_to_all x2, starting transfers between devices: 21.6 us -> 17.1 us  [sent(): return lax.all_to_all(summed, ROW, split_axis=0, concat_axis=0, tiled=True)]
    all_to_all x2, waiting for transfers between devices: 22.3 us -> 25.9 us  [sent(): return lax.all_to_all(summed, ROW, split_axis=0, concat_axis=0, tiled=True)]
    all_gather x1, waiting for transfers between devices: 4.14 us -> 0.79 us  [on_device(): lax.all_gather(pair, 'z', axis=0, tiled=True, axis_index_groups=down)]
    ppermute x1, waiting for transfers between devices: 7.21 us -> 10.5 us  [on_device(): other = lax.ppermute(own, 'yh', [(0, 1), (1, 0)])]
    ppermute x1, starting transfers between devices: 5.16 us -> 3.09 us  [on_device(): other = lax.ppermute(own, 'yh', [(0, 1), (1, 0)])]
where the time goes in v4:
time: 131 us
  blocking collectives  44.3 us (34%)
  waiting for transfers between devices  37.2 us (28%)
  starting transfers between devices  20.2 us (15%)
  between operations  13.5 us (10%)
  Pallas kernels  10.2 us (8%)
  local copies, waits for them, and re-layouts  3.79 us (3%)
  other arithmetic  1.37 us (1%)
    all_gather x1, blocking collectives, on_device(): own = lax.all_gather(early, 'z', axis=0, tiled=True, axis_index_groups=down)  38 us
    all_to_all x2, waiting for transfers between devices, sent(): return lax.all_to_all(summed, ROW, split_axis=0, concat_axis=0, tiled=True)  25.9 us
    all_to_all x2, starting transfers between devices, sent(): return lax.all_to_all(summed, ROW, split_axis=0, concat_axis=0, tiled=True)  17.1 us
    ppermute x1, waiting for transfers between devices, on_device(): other = lax.ppermute(own, 'yh', [(0, 1), (1, 0)])  10.5 us
    pallas_call x2, Pallas kernels, sent(): pl.pallas_call(kernel, out_shape=jax.ShapeDtypeStruct((groups, rows, fine...  7.53 us
    all_gather x1, blocking collectives, on_device(): pair = lax.all_gather(late, 'yh', axis=0, tiled=True)  6.24 us
    unnamed x10, local copies, waits for them, and re-layouts  3.37 us
    ppermute x1, starting transfers between devices, on_device(): other = lax.ppermute(own, 'yh', [(0, 1), (1, 0)])  3.09 us
  transfers between devices with their start and end apart: 4, of which 4 were waited for; matrix products, arithmetic and copies ran while one was open for 3% of the time, Pallas kernels for 7%

profile of v4, /device:TPU:1, one launch (start us, length us, event | category | flops | bytes accessed | tf_op | source)
XLA Modules:
  0.0 130.6 jit_solution(4382345182738009213)
XLA Ops:
  6.5 0.0 all-gather.2.cloned.1.call-start
  6.5 0.0 copy-start
  6.5 0.9 copy-done
  7.4 0.1 shard_map.55
  7.5 6.2 %all_gather.9 = bf16[4,144,128]{2,1,0:T(8,128)(2,1)} all-gather(bf16[2,144,128]{2,1,0:T(8,128)(2,1)S(1)} %get-tuple-element.10), channel_id=1, replica_groups=mesh['yl'=2,'x'=4,'core'=2,'yh'=2,'z'=16] {'yh'}, dimensions={0}, use_global_device_ids=true | all-gather | bytes 221184 | tf_op jit(solution)/shard_map/all_gather | solution.py:177
  13.8 0.0 all-gather.2.cloned.1.call-update
  13.8 38.0 %all_gather.11.own_ref = bf16[32,112,128]{2,1,0:T(8,128)(2,1)S(1)} all-gather(bf16[2,112,128]{2,1,0:T(8,128)(2,1)S(1)} %get-tuple-element.12), channel_id=1, replica_groups={{15,14,13,12,11,10,9,8,7,6,5,4,3,2,1,0},{31,30,29,28,27,26,25,24,23,22,..., dimensions={0}, use_global_device_ids=true | all-gather | bytes 974848 | tf_op jit(solution)/shard_map/all_gather | solution.py:181
  51.8 0.0 copy-start.2
  51.8 3.1 %collective-permute-start = (bf16[32,112,128]{2,1,0:T(8,128)(2,1)S(1)}, bf16[32,112,128]{2,1,0:T(8,128)(2,1)S(1)}, u32[]{:S(2)}, u32[]{:S(2)}) collective-permute-start(bf16[32,112,128]{2,1,0:T(8,128)(2,1)S(1)} %all_gather.11.own_ref), channel_id=1, source_target_pairs={{0,16},{16,0},{1,17},{17,1},{2,18},{18,2},{3,19},{19,3},{4,20},{20... | collective-permute-start | bytes 2752520 | tf_op jit(solution)/shard_map/ppermute | solution.py:182
  54.9 0.8 copy.11
  55.7 0.1 iota_compare_fusion
  55.8 0.1 lt.26
  55.9 0.7 multiply_bitcast_fusion
  56.6 0.1 add.23
  56.6 0.1 add.24
  56.8 0.8 copy.12
  57.5 0.1 reshape.29
  57.6 0.6 pad_add_fusion.table_ref
  58.2 10.5 %collective-permute-done.other_ref = bf16[32,112,128]{2,1,0:T(8,128)(2,1)S(1)} collective-permute-done((bf16[32,112,128]{2,1,0:T(8,128)(2,1)S(1)}, bf16[32,112,128]{2,1,0:T(8,128)(2,1)S(1)}, u32[]{:S(2)}, u32[]{:S(2)}) %collective-permute-start) | collective-permute-done | bytes 917536 | tf_op jit(solution)/shard_map/ppermute | solution.py:182
  68.7 0.0 copy-done.2
  68.7 0.9 copy-done.3
  69.7 3.7 %shard_map.57 = bf16[16,112,256]{2,1,0:T(8,128)(2,1)} custom-call(s32[65]{0:T(128)} %pad_add_fusion.table_ref, bf16[32,112,128]{2,1,0:T(8,128)(2,1)} %copy-done.2, bf16[32,112,128]{2,1,0:T(8,128)(2,1)} %copy-done.3, bf16[32,256,128]{2,1,0:T(8,128)(2,1)} %bitcast.7), custom_call_target="tpu_custom_call" | custom-call | tf_op jit(solution)/shard_map/pallas_call | solution.py:158
  73.4 12.9 %all-to-all-start.1 = ((bf16[16,112,256]{2,1,0:T(8,128)(2,1)}), bf16[16,112,256]{2,1,0:T(8,128)(2,1)S(1)}, u32[]{:S(2)}, u32[]{:S(2)}) async-start(bf16[16,112,256]{2,1,0:T(8,128)(2,1)} %shard_map.57), calls=%async_computation.1 | async-start | bytes 1835008 | tf_op jit(solution)/shard_map/all_to_all | solution.py:175
  86.3 0.8 all-gather.2.cloned.1.call-done.panels_ref
  87.1 3.8 %shard_map.56 = bf16[16,144,256]{2,1,0:T(8,128)(2,1)} custom-call(s32[65]{0:T(128)} %pad_add_fusion.table_ref, bf16[64,144,128]{2,1,0:T(8,128)(2,1)} %all-gather.2.cloned.1.call-done.panels_ref, bf16[32,256,128]{2,1,0:T(8,128)(2,1)} %bitcast.8), custom_call_target="tpu_custom_call" | custom-call | tf_op jit(solution)/shard_map/pallas_call | solution.py:158
  90.9 0.0 copy-start.1
  90.9 9.8 %all-to-all-done.1.t_ref = bf16[16,112,256]{2,1,0:T(8,128)(2,1)S(1)} async-done(((bf16[16,112,256]{2,1,0:T(8,128)(2,1)}), bf16[16,112,256]{2,1,0:T(8,128)(2,1)S(1)}, u32[]{:S(2)}, u32[]{:S(2)}) %all-to-all-start.1) | async-done | bytes 917536 | tf_op jit(solution)/shard_map/all_to_all | solution.py:175
  100.8 4.2 %all-to-all-start = ((bf16[16,144,256]{2,1,0:T(8,128)(2,1)}), bf16[16,144,256]{2,1,0:T(8,128)(2,1)S(1)}, u32[]{:S(2)}, u32[]{:S(2)}) async-start(bf16[16,144,256]{2,1,0:T(8,128)(2,1)} %shard_map.56), calls=%async_computation | async-start | bytes 2359296 | tf_op jit(solution)/shard_map/all_to_all | solution.py:175
  105.0 0.0 copy-done.1
  105.0 1.2 shard_map.58.rest_0_
  106.3 16.1 %all-to-all-done.t_ref = bf16[16,144,256]{2,1,0:T(8,128)(2,1)S(1)} async-done(((bf16[16,144,256]{2,1,0:T(8,128)(2,1)}), bf16[16,144,256]{2,1,0:T(8,128)(2,1)S(1)}, u32[]{:S(2)}, u32[]{:S(2)}) %all-to-all-start) | async-done | bytes 1179680 | tf_op jit(solution)/shard_map/all_to_all | solution.py:175
  122.3 1.4 %shard_map.59 = bf16[16,256,256]{2,1,0:T(8,128)(2,1)} custom-call(bf16[16,144,256]{2,1,0:T(8,128)(2,1)S(1)} %all-to-all-done.t_ref, bf16[256,256]{1,0:T(8,128)(2,1)S(1)} %bitcast.6, bf16[16,256,256]{2,1,0:T(8,128)(2,1)} %shard_map.58.rest_0_), custom_call_target="tpu_custom_call", output_to_operand_aliasing={{}: (2, {})} | custom-call | tf_op jit(solution)/shard_map/pallas_call | solution.py:134
  (2 shorter events, 0.0 us)
Async XLA Ops:
  6.5 80.6 %all-gather.2.cloned.1.call-start = ((), (), s32[]{:S(2)}) async-start(), calls=%async_computation.2 | async-start | bytes 2506752 | tf_op jit(solution)/shard_map/all_gather | solution.py:180
  6.5 0.9 copy-start
  51.8 16.9 %copy-start.2 = (bf16[32,112,128]{2,1,0:T(8,128)(2,1)}, bf16[32,112,128]{2,1,0:T(8,128)(2,1)S(1)}, u32[]{:S(2)}) copy-start(bf16[32,112,128]{2,1,0:T(8,128)(2,1)S(1)} %all_gather.11.own_ref) | copy-start | bytes 2752516
  51.8 16.9 %collective-permute-start = (bf16[32,112,128]{2,1,0:T(8,128)(2,1)S(1)}, bf16[32,112,128]{2,1,0:T(8,128)(2,1)S(1)}, u32[]{:S(2)}, u32[]{:S(2)}) collective-permute-start(bf16[32,112,128]{2,1,0:T(8,128)(2,1)S(1)} %all_gather.11.own_ref), channel_id=1, source_target_pairs={{0,16},{16,0},{1,17},{17,1},{2,18},{18,2},{3,19},{19,3},{4,20},{20... | collective-permute-start | bytes 2752520 | tf_op jit(solution)/shard_map/ppermute | solution.py:182
  68.7 0.9 copy-start.3
  73.4 27.4 %all-to-all-start.1 = ((bf16[16,112,256]{2,1,0:T(8,128)(2,1)}), bf16[16,112,256]{2,1,0:T(8,128)(2,1)S(1)}, u32[]{:S(2)}, u32[]{:S(2)}) async-start(bf16[16,112,256]{2,1,0:T(8,128)(2,1)} %shard_map.57), calls=%async_computation.1 | async-start | bytes 1835008 | tf_op jit(solution)/shard_map/all_to_all | solution.py:175
  90.9 14.1 %copy-start.1 = (bf16[2,128,256]{2,1,0:T(8,128)(2,1)S(1)}, bf16[2,128,256]{2,1,0:T(8,128)(2,1)}, u32[]{:S(2)}) copy-start(bf16[2,128,256]{2,1,0:T(8,128)(2,1)} %p_ref.1) | copy-start | bytes 393220
  100.8 21.6 %all-to-all-start = ((bf16[16,144,256]{2,1,0:T(8,128)(2,1)}), bf16[16,144,256]{2,1,0:T(8,128)(2,1)S(1)}, u32[]{:S(2)}, u32[]{:S(2)}) async-start(bf16[16,144,256]{2,1,0:T(8,128)(2,1)} %shard_map.56), calls=%async_computation | async-start | bytes 2359296 | tf_op jit(solution)/shard_map/all_to_all | solution.py:175
Sparse Core Ops, SparseCore 0:
  13.9 73.1 all-gather.1

commit v5 on v4

--- a/solution.py
+++ b/solution.py
@@ -176,12 +176,13 @@
 
     pair = lax.all_gather(late, "yh", axis=0, tiled=True)
     early, pair = lax.optimization_barrier((early, pair))
-    down = [list(range(side - 1, -1, -1))]
+    start = side + side // 2 - 1
+    down = [[(start - i) % side for i in range(side)]]
     late_panels = lax.all_gather(pair, "z", axis=0, tiled=True, axis_index_groups=down)
     own = lax.all_gather(early, "z", axis=0, tiled=True, axis_index_groups=down)
     other = lax.ppermute(own, "yh", [(0, 1), (1, 0)])
 
-    at = (side - 1 - owner % side) * planes + owner // side
+    at = ((start - owner % side) % side) * planes + owner // side
     at = at.reshape(groups, 1, 1) * fine + row.reshape(groups, fine, -1)
     live = jnp.arange(at.shape[2], dtype=jnp.int32)[None, None] < count[:, :, None]
     here = lax.axis_index("yh").astype(jnp.int32).reshape(1)

time: 131 us -> 131 us (level)
  no operation moved by 1% of the time
where the time goes in v5:
time: 131 us
  blocking collectives  44.3 us (34%)
  waiting for transfers between devices  37.2 us (28%)
  starting transfers between devices  20.2 us (15%)
  between operations  13.5 us (10%)
  Pallas kernels  10.2 us (8%)
  local copies, waits for them, and re-layouts  3.79 us (3%)
  other arithmetic  1.38 us (1%)
    all_gather x1, blocking collectives, on_device(): own = lax.all_gather(early, 'z', axis=0, tiled=True, axis_index_groups=down)  38 us
    all_to_all x2, waiting for transfers between devices, sent(): return lax.all_to_all(summed, ROW, split_axis=0, concat_axis=0, tiled=True)  25.9 us
    all_to_all x2, starting transfers between devices, sent(): return lax.all_to_all(summed, ROW, split_axis=0, concat_axis=0, tiled=True)  17.1 us
    ppermute x1, waiting for transfers between devices, on_device(): other = lax.ppermute(own, 'yh', [(0, 1), (1, 0)])  10.5 us
    pallas_call x2, Pallas kernels, sent(): pl.pallas_call(kernel, out_shape=jax.ShapeDtypeStruct((groups, rows, fine...  7.54 us
    all_gather x1, blocking collectives, on_device(): pair = lax.all_gather(late, 'yh', axis=0, tiled=True)  6.24 us
    unnamed x10, local copies, waits for them, and re-layouts  3.37 us
    ppermute x1, starting transfers between devices, on_device(): other = lax.ppermute(own, 'yh', [(0, 1), (1, 0)])  3.09 us
  transfers between devices with their start and end apart: 4, of which 4 were waited for; matrix products, arithmetic and copies ran while one was open for 3% of the time, Pallas kernels for 7%

profile of v5, /device:TPU:1, one launch (start us, length us, event | category | flops | bytes accessed | tf_op | source)
XLA Modules:
  0.0 130.6 jit_solution(2365629535939887962)
XLA Ops:
  6.5 0.0 all-gather.2.cloned.1.call-start
  6.5 0.0 copy-start
  6.5 0.9 copy-done
  7.4 0.1 shard_map.55
  7.5 6.2 %all_gather.9 = bf16[4,144,128]{2,1,0:T(8,128)(2,1)} all-gather(bf16[2,144,128]{2,1,0:T(8,128)(2,1)S(1)} %get-tuple-element.10), channel_id=1, replica_groups=mesh['yl'=2,'x'=4,'core'=2,'yh'=2,'z'=16] {'yh'}, dimensions={0}, use_global_device_ids=true | all-gather | bytes 221184 | tf_op jit(solution)/shard_map/all_gather | solution.py:177
  13.8 0.0 all-gather.2.cloned.1.call-update
  13.8 38.0 %all_gather.11.own_ref = bf16[32,112,128]{2,1,0:T(8,128)(2,1)S(1)} all-gather(bf16[2,112,128]{2,1,0:T(8,128)(2,1)S(1)} %get-tuple-element.12), channel_id=1, replica_groups={{7,6,5,4,3,2,1,0,15,14,13,12,11,10,9,8},{23,22,21,20,19,18,17,16,31,30,..., dimensions={0}, use_global_device_ids=true | all-gather | bytes 974848 | tf_op jit(solution)/shard_map/all_gather | solution.py:182
  51.8 0.0 copy-start.2
  51.8 3.1 %collective-permute-start = (bf16[32,112,128]{2,1,0:T(8,128)(2,1)S(1)}, bf16[32,112,128]{2,1,0:T(8,128)(2,1)S(1)}, u32[]{:S(2)}, u32[]{:S(2)}) collective-permute-start(bf16[32,112,128]{2,1,0:T(8,128)(2,1)S(1)} %all_gather.11.own_ref), channel_id=1, source_target_pairs={{0,16},{16,0},{1,17},{17,1},{2,18},{18,2},{3,19},{19,3},{4,20},{20... | collective-permute-start | bytes 2752520 | tf_op jit(solution)/shard_map/ppermute | solution.py:183
  54.9 0.8 copy.11
  55.7 0.1 iota_compare_fusion
  55.8 0.1 lt.30
  55.9 0.7 multiply_bitcast_fusion
  56.6 0.1 add.28
  56.6 0.1 add.29
  56.8 0.8 copy.12
  57.5 0.1 reshape.29
  57.6 0.6 pad_add_fusion.table_ref
  58.3 10.5 %collective-permute-done.other_ref = bf16[32,112,128]{2,1,0:T(8,128)(2,1)S(1)} collective-permute-done((bf16[32,112,128]{2,1,0:T(8,128)(2,1)S(1)}, bf16[32,112,128]{2,1,0:T(8,128)(2,1)S(1)}, u32[]{:S(2)}, u32[]{:S(2)}) %collective-permute-start) | collective-permute-done | bytes 917536 | tf_op jit(solution)/shard_map/ppermute | solution.py:183
  68.7 0.0 copy-done.2
  68.7 0.9 copy-done.3
  69.7 3.8 %shard_map.57 = bf16[16,112,256]{2,1,0:T(8,128)(2,1)} custom-call(s32[65]{0:T(128)} %pad_add_fusion.table_ref, bf16[32,112,128]{2,1,0:T(8,128)(2,1)} %copy-done.2, bf16[32,112,128]{2,1,0:T(8,128)(2,1)} %copy-done.3, bf16[32,256,128]{2,1,0:T(8,128)(2,1)} %bitcast.7), custom_call_target="tpu_custom_call" | custom-call | tf_op jit(solution)/shard_map/pallas_call | solution.py:158
  73.4 12.9 %all-to-all-start.1 = ((bf16[16,112,256]{2,1,0:T(8,128)(2,1)}), bf16[16,112,256]{2,1,0:T(8,128)(2,1)S(1)}, u32[]{:S(2)}, u32[]{:S(2)}) async-start(bf16[16,112,256]{2,1,0:T(8,128)(2,1)} %shard_map.57), calls=%async_computation.1 | async-start | bytes 1835008 | tf_op jit(solution)/shard_map/all_to_all | solution.py:175
  86.3 0.8 all-gather.2.cloned.1.call-done.panels_ref
  87.1 3.8 %shard_map.56 = bf16[16,144,256]{2,1,0:T(8,128)(2,1)} custom-call(s32[65]{0:T(128)} %pad_add_fusion.table_ref, bf16[64,144,128]{2,1,0:T(8,128)(2,1)} %all-gather.2.cloned.1.call-done.panels_ref, bf16[32,256,128]{2,1,0:T(8,128)(2,1)} %bitcast.8), custom_call_target="tpu_custom_call" | custom-call | tf_op jit(solution)/shard_map/pallas_call | solution.py:158
  90.9 0.0 copy-start.1
  90.9 9.9 %all-to-all-done.1.t_ref = bf16[16,112,256]{2,1,0:T(8,128)(2,1)S(1)} async-done(((bf16[16,112,256]{2,1,0:T(8,128)(2,1)}), bf16[16,112,256]{2,1,0:T(8,128)(2,1)S(1)}, u32[]{:S(2)}, u32[]{:S(2)}) %all-to-all-start.1) | async-done | bytes 917536 | tf_op jit(solution)/shard_map/all_to_all | solution.py:175
  100.8 4.2 %all-to-all-start = ((bf16[16,144,256]{2,1,0:T(8,128)(2,1)}), bf16[16,144,256]{2,1,0:T(8,128)(2,1)S(1)}, u32[]{:S(2)}, u32[]{:S(2)}) async-start(bf16[16,144,256]{2,1,0:T(8,128)(2,1)} %shard_map.56), calls=%async_computation | async-start | bytes 2359296 | tf_op jit(solution)/shard_map/all_to_all | solution.py:175
  105.0 0.0 copy-done.1
  105.0 1.3 shard_map.58.rest_0_
  106.3 16.1 %all-to-all-done.t_ref = bf16[16,144,256]{2,1,0:T(8,128)(2,1)S(1)} async-done(((bf16[16,144,256]{2,1,0:T(8,128)(2,1)}), bf16[16,144,256]{2,1,0:T(8,128)(2,1)S(1)}, u32[]{:S(2)}, u32[]{:S(2)}) %all-to-all-start) | async-done | bytes 1179680 | tf_op jit(solution)/shard_map/all_to_all | solution.py:175
  122.4 1.4 %shard_map.59 = bf16[16,256,256]{2,1,0:T(8,128)(2,1)} custom-call(bf16[16,144,256]{2,1,0:T(8,128)(2,1)S(1)} %all-to-all-done.t_ref, bf16[256,256]{1,0:T(8,128)(2,1)S(1)} %bitcast.6, bf16[16,256,256]{2,1,0:T(8,128)(2,1)} %shard_map.58.rest_0_), custom_call_target="tpu_custom_call", output_to_operand_aliasing={{}: (2, {})} | custom-call | tf_op jit(solution)/shard_map/pallas_call | solution.py:134
  (2 shorter events, 0.0 us)
Async XLA Ops:
  6.5 80.6 %all-gather.2.cloned.1.call-start = ((), (), s32[]{:S(2)}) async-start(), calls=%async_computation.2 | async-start | bytes 2506752 | tf_op jit(solution)/shard_map/all_gather | solution.py:181
  6.5 0.9 copy-start
  51.8 16.9 %copy-start.2 = (bf16[32,112,128]{2,1,0:T(8,128)(2,1)}, bf16[32,112,128]{2,1,0:T(8,128)(2,1)S(1)}, u32[]{:S(2)}) copy-start(bf16[32,112,128]{2,1,0:T(8,128)(2,1)S(1)} %all_gather.11.own_ref) | copy-start | bytes 2752516
  51.8 16.9 %collective-permute-start = (bf16[32,112,128]{2,1,0:T(8,128)(2,1)S(1)}, bf16[32,112,128]{2,1,0:T(8,128)(2,1)S(1)}, u32[]{:S(2)}, u32[]{:S(2)}) collective-permute-start(bf16[32,112,128]{2,1,0:T(8,128)(2,1)S(1)} %all_gather.11.own_ref), channel_id=1, source_target_pairs={{0,16},{16,0},{1,17},{17,1},{2,18},{18,2},{3,19},{19,3},{4,20},{20... | collective-permute-start | bytes 2752520 | tf_op jit(solution)/shard_map/ppermute | solution.py:183
  68.7 0.9 copy-start.3
  73.4 27.4 %all-to-all-start.1 = ((bf16[16,112,256]{2,1,0:T(8,128)(2,1)}), bf16[16,112,256]{2,1,0:T(8,128)(2,1)S(1)}, u32[]{:S(2)}, u32[]{:S(2)}) async-start(bf16[16,112,256]{2,1,0:T(8,128)(2,1)} %shard_map.57), calls=%async_computation.1 | async-start | bytes 1835008 | tf_op jit(solution)/shard_map/all_to_all | solution.py:175
  90.9 14.1 %copy-start.1 = (bf16[2,128,256]{2,1,0:T(8,128)(2,1)S(1)}, bf16[2,128,256]{2,1,0:T(8,128)(2,1)}, u32[]{:S(2)}) copy-start(bf16[2,128,256]{2,1,0:T(8,128)(2,1)} %p_ref.1) | copy-start | bytes 393220
  100.8 21.6 %all-to-all-start = ((bf16[16,144,256]{2,1,0:T(8,128)(2,1)}), bf16[16,144,256]{2,1,0:T(8,128)(2,1)S(1)}, u32[]{:S(2)}, u32[]{:S(2)}) async-start(bf16[16,144,256]{2,1,0:T(8,128)(2,1)} %shard_map.56), calls=%async_computation | async-start | bytes 2359296 | tf_op jit(solution)/shard_map/all_to_all | solution.py:175
Sparse Core Ops, SparseCore 0:
  13.9 73.1 all-gather.1
